TPU v7x, 512 devices: a whole 4x8x8 slice. The times are simulated.
512 devices in a mesh: row: 64 (over y, z), col: 8 (over x, core).
Axes of the slice: x: 4, y: 8, z: 8, core: 2. Of those that a mesh axis runs over, the one named last changes fastest.
Arguments:
- features: bfloat16 [65536, 512], P(('row', 'col')), may hold values from -6 to 6
- weight: bfloat16 [512, 512], replicated, may hold values from -0.25 to 0.25
- bias_vec: float32 [512], replicated, may hold values from -3 to 3
- tile_vals: bfloat16 [64, 8, 16, 128, 128], P('row', 'col'), may hold values from -0.1875 to 0.1875
- tile_coords: int32 [64, 8, 16, 2], P('row', 'col'), may hold values from 0 to 63, as said below
- tile_count: int32 [64, 8], P('row', 'col'), may hold values from 2 to 16, as said below
- cotangent: bfloat16 [65536, 512], P(('row', 'col')), may hold values from -6 to 6
Outputs:
- layer_out: bfloat16 [65536, 512], P(('row', 'col'))
- grad_weight: float32 [512, 512], replicated
- grad_bias: float32 [512], replicated
- grad_features: bfloat16 [65536, 512], P(('row', 'col'))
Inputs may be any that keep to these rules, and one draw needn't show every extreme that they name: tile_coords[r, c, s, 0] is below 8; tile_coords[r, c, s, 1] lies in the row bands r - 3 to r + 3 that exist. `tile_count`: some device has all 16 slots live.
All inputs are finite; a program needn't handle non-finite values.
Results may differ from a plain program's by a relative error of at most 0.019.
Values may be sent and summed in bfloat16 or wider, within the bound.
No kernel may reach another device: no remote copies, remote signals or barrier semaphores. Data moves between devices by JAX's collectives and lax.ppermute only.
A program may use at most 64 MiB of HBM per device.

v0:
```python
import jax
import jax.numpy as jnp
from jax import lax
from jax.sharding import PartitionSpec as P

REACH = 3


def passed_along(block, axis, distance):
    devices = range(lax.axis_size(axis))
    route = [(i - distance, i) for i in devices if i - distance in devices]
    return lax.ppermute(block, axis, route)


def gelu_tanh(values):
    return jax.nn.gelu(values, approximate=True)


def body(features, weight, bias_vec, tile_vals, tile_coords, tile_count, cotangent):
    col_count = lax.axis_size("col")
    own_row = lax.axis_index("row")
    tiles_here = tile_vals[0, 0]
    coords_here = tile_coords[0, 0]
    live_count = tile_count[0, 0]
    slot_count = tiles_here.shape[0]
    tile_size = features.shape[0]
    feat_width = features.shape[1]
    window = 2 * REACH + 1
    per_step = 8
    row_local = coords_here[:, 0]
    col_local = coords_here[:, 1]
    alive_mask = (jnp.arange(slot_count, dtype=jnp.int32) < live_count).astype(jnp.float32)
    window_index = col_local - own_row + REACH
    nearby = []
    for shift_by in range(-REACH, REACH + 1):
        if shift_by == 0:
            nearby.append(features)
        else:
            nearby.append(passed_along(features, "row", -shift_by))
    panels = jnp.stack(nearby)
    step_total = slot_count // per_step

    def slot_slices(group_idx):
        first_slot = group_idx * per_step
        tiles_now = lax.dynamic_slice_in_dim(tiles_here, first_slot, per_step, 0)
        alive_now = lax.dynamic_slice_in_dim(alive_mask, first_slot, per_step, 0)
        return (first_slot, tiles_now, alive_now)

    def forward_group(group_idx, totals):
        first_slot, tiles_now, alive_now = slot_slices(group_idx)
        col_pick = lax.dynamic_slice_in_dim(window_index, first_slot, per_step, 0)
        row_pick = lax.dynamic_slice_in_dim(row_local, first_slot, per_step, 0)
        picked = panels[col_pick]
        product = jnp.einsum("gij,gjf->gif", tiles_now, picked, preferred_element_type=jnp.float32)
        onehot = (row_pick[:, None] == jnp.arange(col_count, dtype=jnp.int32)[None, :]).astype(
            jnp.float32
        )
        onehot = onehot * alive_now[:, None]
        return totals + jnp.einsum("gb,gif->bif", onehot, product)

    partial_value = lax.fori_loop(
        0, step_total, forward_group, jnp.zeros((col_count, tile_size, feat_width), jnp.float32)
    )
    aggregate = lax.psum_scatter(
        partial_value.reshape(col_count * tile_size, feat_width),
        "col",
        scatter_dimension=0,
        tiled=True,
    )
    aggregate_b = aggregate.astype(jnp.bfloat16)
    pre_act = jnp.dot(aggregate_b, weight, preferred_element_type=jnp.float32) + bias_vec
    layer_out = gelu_tanh(pre_act).astype(jnp.bfloat16)
    unused_out, pullback = jax.vjp(gelu_tanh, pre_act)
    grad_pre = pullback(cotangent.astype(jnp.float32))[0].astype(jnp.bfloat16)
    weight_term = jnp.einsum("nf,ng->fg", aggregate_b, grad_pre, preferred_element_type=jnp.float32)
    bias_term = jnp.sum(grad_pre.astype(jnp.float32), axis=0)
    grad_weight, grad_bias = lax.psum((weight_term, bias_term), ("row", "col"))
    grad_mid = jnp.einsum("ng,fg->nf", grad_pre, weight, preferred_element_type=jnp.float32).astype(
        jnp.bfloat16
    )
    band_panels = lax.all_gather(grad_mid, "col", axis=0, tiled=True).reshape(
        col_count, tile_size, feat_width
    )

    def backward_group(group_idx, totals):
        first_slot, tiles_now, alive_now = slot_slices(group_idx)
        row_pick = lax.dynamic_slice_in_dim(row_local, first_slot, per_step, 0)
        win_pick = lax.dynamic_slice_in_dim(window_index, first_slot, per_step, 0)
        picked = band_panels[row_pick]
        product = jnp.einsum("gji,gjf->gif", tiles_now, picked, preferred_element_type=jnp.float32)
        onehot = (win_pick[:, None] == jnp.arange(window, dtype=jnp.int32)[None, :]).astype(
            jnp.float32
        )
        onehot = onehot * alive_now[:, None]
        return totals + jnp.einsum("gb,gif->bif", onehot, product)

    grad_acc = lax.fori_loop(
        0, step_total, backward_group, jnp.zeros((window, tile_size, feat_width), jnp.float32)
    )
    result_sum = grad_acc[REACH]
    for shift_by in range(-REACH, REACH + 1):
        if shift_by != 0:
            result_sum = result_sum + passed_along(grad_acc[shift_by + REACH], "row", shift_by)
    grad_features = result_sum.astype(jnp.bfloat16)
    return (layer_out, grad_weight, grad_bias, grad_features)


def solution(mesh):
    return jax.shard_map(
        body,
        mesh=mesh,
        in_specs=(
            P(("row", "col"), None),
            P(),
            P(),
            P("row", "col", None, None, None),
            P("row", "col", None, None),
            P("row", "col"),
            P(("row", "col"), None),
        ),
        out_specs=(P(("row", "col"), None), P(), P(), P(("row", "col"), None)),
        check_vma=False,
    )
```

profile of v0, /device:TPU:24, one launch (start us, length us, event | category | flops | bytes accessed | tf_op | source)
XLA Modules:
  0.0 473.3 jit_solution(12974934062237815644)
XLA Ops:
  7.2 0.0 copy-start
  7.2 0.0 reduce-scatter.2.cloned.1.call-start
  7.2 8.0 %collective-permute-start = (bf16[128,512]{1,0:T(8,128)(2,1)}, bf16[128,512]{1,0:T(8,128)(2,1)S(1)}, u32[]{:S(2)}, u32[]{:S(2)}) collective-permute-start(bf16[128,512]{1,0:T(8,128)(2,1)} %param.11), channel_id=1, source_target_pairs={{0,24},{8,32},{16,40},{24,48},{32,56},{40,64},{48,72},{56,80},{64,... | collective-permute-start | bytes 393224 | tf_op jit(solution)/shard_map/ppermute | solution.py:12
  15.3 6.4 %collective-permute-start.1 = (bf16[128,512]{1,0:T(8,128)(2,1)}, bf16[128,512]{1,0:T(8,128)(2,1)S(1)}, u32[]{:S(2)}, u32[]{:S(2)}) collective-permute-start(bf16[128,512]{1,0:T(8,128)(2,1)} %param.11), channel_id=1, source_target_pairs={{0,16},{8,24},{16,32},{24,40},{32,48},{40,56},{48,64},{56,72},{64,... | collective-permute-start | bytes 393224 | tf_op jit(solution)/shard_map/ppermute | solution.py:12
  21.7 3.4 collective-permute-start.2
  25.1 4.6 collective-permute-start.3
  29.6 1.9 collective-permute-start.4
  31.6 0.8 add_bitcast_fusion
  33.0 4.2 collective-permute-start.5
  37.2 0.0 collective-permute-done.1
  37.3 0.9 bitcast_dynamic-update-slice_fusion.3
  38.2 2.6 collective-permute-done.4
  40.9 11.6 %collective-permute-done.5 = bf16[128,512]{1,0:T(8,128)(2,1)S(1)} collective-permute-done((bf16[128,512]{1,0:T(8,128)(2,1)}, bf16[128,512]{1,0:T(8,128)(2,1)S(1)}, u32[]{:S(2)}, u32[]{:S(2)}) %collective-permute-start.5) | collective-permute-done | bytes 131104 | tf_op jit(solution)/shard_map/ppermute | solution.py:12
  52.5 10.2 %while.28 = (s32[]{:T(128)}, f32[8,128,512]{2,0,1:T(8,128)}, s32[16]{0:T(128)S(1)}, bf16[16]{0:T(256)(128)(2,1)S(1)}, bf16[16,128,128]{2,1,0:T(8,128)(2,1)}, /*i...) while((s32[]{:T(128)}, f32[8,128,512]{2,0,1:T(8,128)}, ...), condition=%wide.region_1.0_spmd.clone, body=%wide.region_0.0_spmd.clone.sunk | while | flops 143656096 | bytes 9703877 | solution.py:61
  52.5 0.1 compare_select_fusion.4
  52.6 0.6 gather_fusion
  53.2 1.4 fusion.67
  54.6 0.1 dynamic_slice.80
  54.7 0.1 dynamic_slice.81
  54.7 2.1 select_add_fusion.4
  56.8 0.1 compare_select_fusion.4
  56.9 0.6 gather_fusion
  57.5 1.4 fusion.67
  58.9 0.1 dynamic_slice.80
  59.0 0.1 dynamic_slice.81
  59.1 3.7 select_add_fusion.4
  62.7 4.1 copy.18
  66.9 0.0 reduce-scatter.2.cloned.1.call-update
  66.9 0.0 all-gather.2.cloned.1.call-start
  67.0 33.2 %reduce-scatter.2.cloned.1.call-done = f32[128,512]{1,0:T(8,128)} async-done(((f32[1024,512]{1,0:T(8,128)}), f32[128,512]{1,0:T(8,128)}) %reduce-scatter.2.cloned.1.call-update) | async-done | bytes 262160 | tf_op jit(solution)/shard_map/reduce_scatter | solution.py:64
  100.2 2.0 convert_reduce_fusion
  102.2 1.0 convolution_convert_fusion
  103.2 0.0 all-gather.2.cloned.1.call-update
  103.2 0.0 all-reduce.2.cloned.1.call-start
  103.2 27.5 %all-gather.2.cloned.1.call-done = bf16[1024,512]{1,0:T(8,128)(2,1)} async-done(((bf16[128,512]{1,0:T(8,128)(2,1)}), bf16[1024,512]{1,0:T(8,128)(2,1)}) %all-gather.2.cloned.1.call-update) | async-done | bytes 1048592 | tf_op jit(solution)/shard_map/all_gather | solution.py:81
  130.8 11.0 %while.29 = (s32[]{:T(128)}, f32[7,128,512]{2,0,1:T(8,128)}, s32[16]{0:T(128)S(1)}, bf16[16]{0:T(256)(128)(2,1)S(1)}, bf16[16,128,128]{2,1,0:T(8,128)(2,1)S(1)},...) while((s32[]{:T(128)}, f32[7,128,512]{2,0,1:T(8,128)}, ...), condition=%wide.region_7.0_spmd.clone, body=%wide.region_6.0_spmd.clone.sunk | while | flops 142476432 | bytes 9179589 | solution.py:97
  130.8 0.1 compare_select_fusion.5
  130.9 1.8 gather_fusion.1
  132.7 0.5 fusion.72
  133.2 0.1 dynamic_slice.84
  133.3 0.1 dynamic_slice.85
  133.4 2.1 select_add_fusion.5
  135.5 0.1 compare_select_fusion.5
  135.6 1.8 gather_fusion.1
  137.4 0.5 fusion.72
  137.9 0.1 dynamic_slice.84
  138.0 0.1 dynamic_slice.85
  138.1 3.7 select_add_fusion.5
  141.8 2.7 copy.19
  144.5 1.0 slice_bitcast_fusion.5
  145.4 4.6 collective-permute-start.10
  150.1 6.0 %collective-permute-start.11 = (f32[128,512]{1,0:T(8,128)}, f32[128,512]{1,0:T(8,128)S(1)}, u32[]{:S(2)}, u32[]{:S(2)}) collective-permute-start(f32[128,512]{1,0:T(8,128)} %get-tuple-element.333), channel_id=1, source_target_pairs={{0,24},{8,32},{16,40},{24,48},{32,56},{40,64},{48,72},{56,80},{64,... | collective-permute-start | bytes 786440 | tf_op jit(solution)/shard_map/ppermute | solution.py:12
  156.1 3.7 collective-permute-start.6
  159.8 3.3 collective-permute-start.7
  163.2 3.7 collective-permute-start.8
  166.9 1.6 collective-permute-done.10
  168.5 3.8 collective-permute-start.9
  172.4 1.3 fusion.43
  173.7 0.0 all-reduce.2.cloned.1.call-update
  173.7 123.1 %psum.15 = f32[512]{0:T(512)} all-reduce(f32[512]{0:T(512)S(1)} %get-tuple-element.330), channel_id=1, replica_groups=mesh['row'=64,'col'=8] {'row','col'}, use_global_device_ids=true, to_apply=%region_5.0 | all-reduce | flops 512 | bytes 4096 | tf_op jit(solution)/shard_map/psum | solution.py:77
  296.8 0.0 collective-permute-done.11
  296.9 2.0 fusion.42
  298.9 165.6 %all-reduce.2.cloned.1.call-done = f32[512,512]{1,0:T(8,128)} async-done(((f32[512,512]{1,0:T(8,128)}), f32[512,512]{1,0:T(8,128)}) %all-reduce.2.cloned.1.call-update) | async-done | bytes 1048592 | tf_op jit(solution)/shard_map/psum | solution.py:77
  464.5 2.3 copy.60
  (29 shorter events, 0.1 us)
Async XLA Ops:
  7.2 93.0 %copy-start = (bf16[512,512]{1,0:T(8,128)(2,1)S(1)}, bf16[512,512]{1,0:T(8,128)(2,1)}, u32[]{:S(2)}) copy-start(bf16[512,512]{1,0:T(8,128)(2,1)} %param.12) | copy-start | bytes 1572868
  7.2 93.0 %reduce-scatter.2.cloned.1.call-start = ((), (), s32[]{:S(2)}) async-start(), calls=%async_computation.1 | async-start | bytes 2359296 | tf_op jit(solution)/shard_map/reduce_scatter | solution.py:64
  7.2 25.8 %collective-permute-start = (bf16[128,512]{1,0:T(8,128)(2,1)}, bf16[128,512]{1,0:T(8,128)(2,1)S(1)}, u32[]{:S(2)}, u32[]{:S(2)}) collective-permute-start(bf16[128,512]{1,0:T(8,128)(2,1)} %param.11), channel_id=1, source_target_pairs={{0,24},{8,32},{16,40},{24,48},{32,56},{40,64},{48,72},{56,80},{64,... | collective-permute-start | bytes 393224 | tf_op jit(solution)/shard_map/ppermute | solution.py:12
  15.3 22.0 %collective-permute-start.1 = (bf16[128,512]{1,0:T(8,128)(2,1)}, bf16[128,512]{1,0:T(8,128)(2,1)S(1)}, u32[]{:S(2)}, u32[]{:S(2)}) collective-permute-start(bf16[128,512]{1,0:T(8,128)(2,1)} %param.11), channel_id=1, source_target_pairs={{0,16},{8,24},{16,32},{24,40},{32,48},{40,56},{48,64},{56,72},{64,... | collective-permute-start | bytes 393224 | tf_op jit(solution)/shard_map/ppermute | solution.py:12
  21.7 15.6 %collective-permute-start.2 = (bf16[128,512]{1,0:T(8,128)(2,1)}, bf16[128,512]{1,0:T(8,128)(2,1)S(1)}, u32[]{:S(2)}, u32[]{:S(2)}) collective-permute-start(bf16[128,512]{1,0:T(8,128)(2,1)} %param.11), channel_id=1, source_target_pairs={{0,8},{8,16},{16,24},{24,32},{32,40},{40,48},{48,56},{56,64},{64,7... | collective-permute-start | bytes 393224 | tf_op jit(solution)/shard_map/ppermute | solution.py:12
  25.1 13.1 %collective-permute-start.3 = (bf16[128,512]{1,0:T(8,128)(2,1)}, bf16[128,512]{1,0:T(8,128)(2,1)S(1)}, u32[]{:S(2)}, u32[]{:S(2)}) collective-permute-start(bf16[128,512]{1,0:T(8,128)(2,1)} %param.11), channel_id=1, source_target_pairs={{8,0},{16,8},{24,16},{32,24},{40,32},{48,40},{56,48},{64,56},{72,6... | collective-permute-start | bytes 393224 | tf_op jit(solution)/shard_map/ppermute | solution.py:12
  29.6 11.2 %collective-permute-start.4 = (bf16[128,512]{1,0:T(8,128)(2,1)}, bf16[128,512]{1,0:T(8,128)(2,1)S(1)}, u32[]{:S(2)}, u32[]{:S(2)}) collective-permute-start(bf16[128,512]{1,0:T(8,128)(2,1)} %param.11), channel_id=1, source_target_pairs={{16,0},{24,8},{32,16},{40,24},{48,32},{56,40},{64,48},{72,56},{80,... | collective-permute-start | bytes 393224 | tf_op jit(solution)/shard_map/ppermute | solution.py:12
  33.0 19.5 %collective-permute-start.5 = (bf16[128,512]{1,0:T(8,128)(2,1)}, bf16[128,512]{1,0:T(8,128)(2,1)S(1)}, u32[]{:S(2)}, u32[]{:S(2)}) collective-permute-start(bf16[128,512]{1,0:T(8,128)(2,1)} %param.11), channel_id=1, source_target_pairs={{24,0},{32,8},{40,16},{48,24},{56,32},{64,40},{72,48},{80,56},{88,... | collective-permute-start | bytes 393224 | tf_op jit(solution)/shard_map/ppermute | solution.py:12
  66.9 33.3 %copy-start.3 = (bf16[128,512]{1,0:T(8,128)(2,1)S(1)}, bf16[128,512]{1,0:T(8,128)(2,1)}, u32[]{:S(2)}) copy-start(bf16[128,512]{1,0:T(8,128)(2,1)} %param.17) | copy-start | bytes 393220
  66.9 33.3 %copy-start.4 = (f32[512]{0:T(512)S(1)}, f32[512]{0:T(512)}, u32[]{:S(2)}) copy-start(f32[512]{0:T(512)} %param.13) | copy-start | bytes 6148
  66.9 63.9 %copy-start.1 = (bf16[16,128,128]{2,1,0:T(8,128)(2,1)S(1)}, bf16[16,128,128]{2,1,0:T(8,128)(2,1)}, u32[]{:S(2)}) copy-start(bf16[16,128,128]{2,1,0:T(8,128)(2,1)} %get-tuple-element.501) | copy-start | bytes 1572868
  66.9 63.9 %all-gather.2.cloned.1.call-start = ((), (), s32[]{:S(2)}) async-start(), calls=%async_computation.3 | async-start | bytes 1179648 | tf_op jit(solution)/shard_map/all_gather | solution.py:81
  103.2 361.3 %all-reduce.2.cloned.1.call-start = ((), (), s32[]{:S(2)}) async-start(), calls=%async_computation.2 | async-start | bytes 2097152 | tf_op jit(solution)/shard_map/psum | solution.py:77
  144.5 27.9 %copy-start.2 = (f32[128,512]{1,0:T(8,128)S(1)}, f32[128,512]{1,0:T(8,128)}, u32[]{:S(2)}) copy-start(f32[128,512]{1,0:T(8,128)} %reduce-scatter.2.cloned.1.call-done) | copy-start | bytes 786436
  145.4 23.1 %collective-permute-start.10 = (f32[128,512]{1,0:T(8,128)S(1)}, f32[128,512]{1,0:T(8,128)S(1)}, u32[]{:S(2)}, u32[]{:S(2)}) collective-permute-start(f32[128,512]{1,0:T(8,128)S(1)} %get-tuple-element.334), channel_id=1, source_target_pairs={{0,16},{8,24},{16,32},{24,40},{32,48},{40,56},{48,64},{56,72},{64,... | collective-permute-start | bytes 786440 | tf_op jit(solution)/shard_map/ppermute | solution.py:12
  150.1 146.8 %collective-permute-start.11 = (f32[128,512]{1,0:T(8,128)}, f32[128,512]{1,0:T(8,128)S(1)}, u32[]{:S(2)}, u32[]{:S(2)}) collective-permute-start(f32[128,512]{1,0:T(8,128)} %get-tuple-element.333), channel_id=1, source_target_pairs={{0,24},{8,32},{16,40},{24,48},{32,56},{40,64},{48,72},{56,80},{64,... | collective-permute-start | bytes 786440 | tf_op jit(solution)/shard_map/ppermute | solution.py:12
  156.1 140.7 %collective-permute-start.6 = (f32[128,512]{1,0:T(8,128)}, f32[128,512]{1,0:T(8,128)}, u32[]{:S(2)}, u32[]{:S(2)}) collective-permute-start(f32[128,512]{1,0:T(8,128)} %get-tuple-element.332), channel_id=1, source_target_pairs={{24,0},{32,8},{40,16},{48,24},{56,32},{64,40},{72,48},{80,56},{88,... | collective-permute-start | bytes 786440 | tf_op jit(solution)/shard_map/ppermute | solution.py:12
  159.8 137.0 %collective-permute-start.7 = (f32[128,512]{1,0:T(8,128)}, f32[128,512]{1,0:T(8,128)}, u32[]{:S(2)}, u32[]{:S(2)}) collective-permute-start(f32[128,512]{1,0:T(8,128)} %get-tuple-element.337), channel_id=1, source_target_pairs={{16,0},{24,8},{32,16},{40,24},{48,32},{56,40},{64,48},{72,56},{80,... | collective-permute-start | bytes 786440 | tf_op jit(solution)/shard_map/ppermute | solution.py:12
  163.2 133.7 %collective-permute-start.8 = (f32[128,512]{1,0:T(8,128)S(1)}, f32[128,512]{1,0:T(8,128)}, u32[]{:S(2)}, u32[]{:S(2)}) collective-permute-start(f32[128,512]{1,0:T(8,128)S(1)} %get-tuple-element.336), channel_id=1, source_target_pairs={{8,0},{16,8},{24,16},{32,24},{40,32},{48,40},{56,48},{64,56},{72,6... | collective-permute-start | bytes 786440 | tf_op jit(solution)/shard_map/ppermute | solution.py:12
  168.5 128.3 %collective-permute-start.9 = (f32[128,512]{1,0:T(8,128)S(1)}, f32[128,512]{1,0:T(8,128)}, u32[]{:S(2)}, u32[]{:S(2)}) collective-permute-start(f32[128,512]{1,0:T(8,128)S(1)} %get-tuple-element.335), channel_id=1, source_target_pairs={{0,8},{8,16},{16,24},{24,32},{32,40},{40,48},{48,56},{56,64},{64,7... | collective-permute-start | bytes 786440 | tf_op jit(solution)/shard_map/ppermute | solution.py:12
Sparse Core Ops, SparseCore 0:
  67.0 33.0 reduce-scatter.1
  103.3 27.4 all-gather.1
  173.8 290.6 all-reduce.1
where the time goes:
time: 474 us; the launch traced here: 473 us
  waiting for transfers between devices  242 us (51%)
  blocking collectives  123 us (26%)
  starting transfers between devices  53.9 us (11%)
  matrix products  19.6 us (4%)
  local copies, waits for them, and re-layouts  16.5 us (3%)
  between operations  14.6 us (3%)
    psum x1, waiting for transfers between devices, body(): grad_weight, grad_bias = lax.psum((weight_term, bias_term), ('row', 'col'))  166 us
    psum x1, blocking collectives, body(): grad_weight, grad_bias = lax.psum((weight_term, bias_term), ('row', 'col'))  123 us
    ppermute x12, starting transfers between devices, passed_along(): return lax.ppermute(block, axis, route)  53.8 us
    reduce_scatter x1, waiting for transfers between devices, body(): lax.psum_scatter(partial_value.reshape(col_count * tile_size, feat_width)...  33.2 us
    all_gather x1, waiting for transfers between devices, body(): lax.all_gather(grad_mid, 'col', axis=0, tiled=True)  27.5 us
    ppermute x12, waiting for transfers between devices, passed_along(): return lax.ppermute(block, axis, route)  15.9 us
  transfers between devices with their start and end apart: 15, of which 6 were waited for; matrix products, arithmetic and copies ran while one was open for 1% of the time, Pallas kernels for 0%

commit v1 on v0

--- a/solution.py
+++ b/solution.py
@@ -74,7 +74,7 @@
     grad_pre = pullback(cotangent.astype(jnp.float32))[0].astype(jnp.bfloat16)
     weight_term = jnp.einsum("nf,ng->fg", aggregate_b, grad_pre, preferred_element_type=jnp.float32)
     bias_term = jnp.sum(grad_pre.astype(jnp.float32), axis=0)
-    grad_weight, grad_bias = lax.psum((weight_term, bias_term), ("row", "col"))
+    grad_weight, grad_bias = lax.psum(lax.psum((weight_term, bias_term), "col"), "row")
     grad_mid = jnp.einsum("ng,fg->nf", grad_pre, weight, preferred_element_type=jnp.float32).astype(
         jnp.bfloat16
     )

time: 474 us -> 431 us (0.909)
  the two profiles are of different devices: /device:TPU:24 before, /device:TPU:32 now
where the time goes in v1:
time: 431 us; the launch traced here: 430 us
  blocking collectives  172 us (40%)
  waiting for transfers between devices  152 us (35%)
  starting transfers between devices  52 us (12%)
  matrix products  19.7 us (5%)
  local copies, waits for them, and re-layouts  16.5 us (4%)
  between operations  14.7 us (3%)
    psum x1, blocking collectives, body(): lax.psum(lax.psum((weight_term, bias_term), 'col'), 'row')  159 us
    psum x1, waiting for transfers between devices, body(): lax.psum((weight_term, bias_term), 'col')  71.1 us
    ppermute x12, starting transfers between devices, passed_along(): return lax.ppermute(block, axis, route)  51.8 us
    reduce_scatter x1, waiting for transfers between devices, body(): lax.psum_scatter(partial_value.reshape(col_count * tile_size, feat_width)...  35 us
    all_gather x1, waiting for transfers between devices, body(): lax.all_gather(grad_mid, 'col', axis=0, tiled=True)  30.8 us
    ppermute x12, waiting for transfers between devices, passed_along(): return lax.ppermute(block, axis, route)  15.1 us
    psum x1, blocking collectives, body(): lax.psum((weight_term, bias_term), 'col')  13.2 us
  transfers between devices with their start and end apart: 16, of which 5 were waited for; matrix products, arithmetic and copies ran while one was open for 4% of the time, Pallas kernels for 0%

profile of v1, /device:TPU:32, one launch (start us, length us, event | category | flops | bytes accessed | tf_op | source)
XLA Modules:
  0.0 430.2 jit_solution(12899982540576874349)
XLA Ops:
  7.2 0.0 copy-start
  7.2 0.0 reduce-scatter.2.cloned.1.call-start
  7.2 8.0 %collective-permute-start = (bf16[128,512]{1,0:T(8,128)(2,1)}, bf16[128,512]{1,0:T(8,128)(2,1)S(1)}, u32[]{:S(2)}, u32[]{:S(2)}) collective-permute-start(bf16[128,512]{1,0:T(8,128)(2,1)} %param.11), channel_id=1, source_target_pairs={{0,24},{8,32},{16,40},{24,48},{32,56},{40,64},{48,72},{56,80},{64,... | collective-permute-start | bytes 393224 | tf_op jit(solution)/shard_map/ppermute | solution.py:12
  15.3 6.4 %collective-permute-start.1 = (bf16[128,512]{1,0:T(8,128)(2,1)}, bf16[128,512]{1,0:T(8,128)(2,1)S(1)}, u32[]{:S(2)}, u32[]{:S(2)}) collective-permute-start(bf16[128,512]{1,0:T(8,128)(2,1)} %param.11), channel_id=1, source_target_pairs={{0,16},{8,24},{16,32},{24,40},{32,48},{40,56},{48,64},{56,72},{64,... | collective-permute-start | bytes 393224 | tf_op jit(solution)/shard_map/ppermute | solution.py:12
  21.7 3.4 collective-permute-start.2
  25.1 5.8 %collective-permute-start.3 = (bf16[128,512]{1,0:T(8,128)(2,1)}, bf16[128,512]{1,0:T(8,128)(2,1)S(1)}, u32[]{:S(2)}, u32[]{:S(2)}) collective-permute-start(bf16[128,512]{1,0:T(8,128)(2,1)} %param.11), channel_id=1, source_target_pairs={{8,0},{16,8},{24,16},{32,24},{40,32},{48,40},{56,48},{64,56},{72,6... | collective-permute-start | bytes 393224 | tf_op jit(solution)/shard_map/ppermute | solution.py:12
  30.9 1.9 collective-permute-start.4
  32.8 0.8 add_bitcast_fusion
  34.2 3.0 collective-permute-start.5
  37.3 0.9 bitcast_dynamic-update-slice_fusion.3
  38.2 12.3 %collective-permute-done.4 = bf16[128,512]{1,0:T(8,128)(2,1)S(1)} collective-permute-done((bf16[128,512]{1,0:T(8,128)(2,1)}, bf16[128,512]{1,0:T(8,128)(2,1)S(1)}, u32[]{:S(2)}, u32[]{:S(2)}) %collective-permute-start.4) | collective-permute-done | bytes 131104 | tf_op jit(solution)/shard_map/ppermute | solution.py:12
  50.5 10.3 %while.28 = (s32[]{:T(128)}, f32[8,128,512]{2,0,1:T(8,128)}, s32[16]{0:T(128)S(1)}, bf16[16]{0:T(256)(128)(2,1)S(1)}, bf16[16,128,128]{2,1,0:T(8,128)(2,1)}, /*i...) while((s32[]{:T(128)}, f32[8,128,512]{2,0,1:T(8,128)}, ...), condition=%wide.region_1.0_spmd.clone, body=%wide.region_0.0_spmd.clone.sunk | while | flops 143656096 | bytes 9703877 | solution.py:61
  50.5 0.1 compare_select_fusion.4
  50.6 0.6 gather_fusion
  51.3 1.4 fusion.67
  52.6 0.1 dynamic_slice.80
  52.7 0.1 dynamic_slice.81
  52.8 2.1 select_add_fusion.4
  54.9 0.1 compare_select_fusion.4
  55.0 0.6 gather_fusion
  55.6 1.4 fusion.67
  57.0 0.1 dynamic_slice.80
  57.1 0.1 dynamic_slice.81
  57.1 3.7 select_add_fusion.4
  60.8 4.1 copy.18
  65.0 0.0 reduce-scatter.2.cloned.1.call-update
  65.0 0.0 all-reduce.3.cloned.1.call-start
  65.0 35.0 %reduce-scatter.2.cloned.1.call-done = f32[128,512]{1,0:T(8,128)} async-done(((f32[1024,512]{1,0:T(8,128)}), f32[128,512]{1,0:T(8,128)}) %reduce-scatter.2.cloned.1.call-update) | async-done | bytes 262160 | tf_op jit(solution)/shard_map/reduce_scatter | solution.py:64
  100.0 2.1 convert_reduce_fusion
  102.1 1.3 fusion.43
  103.4 0.0 all-reduce.3.cloned.1.call-update
  103.4 0.0 all-gather.2.cloned.1.call-start
  103.5 1.0 convolution_convert_fusion
  104.4 0.0 all-gather.2.cloned.1.call-update
  104.5 0.0 all-reduce.5.cloned.1.call-start
  104.5 71.1 %all-reduce.3.cloned.1.call-done = f32[512,512]{1,0:T(8,128)} async-done(((f32[512,512]{1,0:T(8,128)}), f32[512,512]{1,0:T(8,128)}) %all-reduce.3.cloned.1.call-update) | async-done | bytes 1048592 | tf_op jit(solution)/shard_map/psum | solution.py:77
  175.6 0.0 all-reduce.5.cloned.1.call-update
  175.6 30.8 %all-gather.2.cloned.1.call-done = bf16[1024,512]{1,0:T(8,128)(2,1)} async-done(((bf16[128,512]{1,0:T(8,128)(2,1)}), bf16[1024,512]{1,0:T(8,128)(2,1)}) %all-gather.2.cloned.1.call-update) | async-done | bytes 1048592 | tf_op jit(solution)/shard_map/all_gather | solution.py:81
  206.4 11.0 %while.29 = (s32[]{:T(128)}, f32[7,128,512]{2,0,1:T(8,128)}, s32[16]{0:T(128)S(1)}, bf16[16]{0:T(256)(128)(2,1)S(1)}, bf16[16,128,128]{2,1,0:T(8,128)(2,1)S(1)},...) while((s32[]{:T(128)}, f32[7,128,512]{2,0,1:T(8,128)}, ...), condition=%wide.region_9.0_spmd.clone, body=%wide.region_8.0_spmd.clone.sunk | while | flops 142476432 | bytes 9179589 | solution.py:97
  206.4 0.1 compare_select_fusion.5
  206.5 1.8 gather_fusion.1
  208.4 0.5 fusion.72
  208.9 0.1 dynamic_slice.84
  209.0 0.1 dynamic_slice.85
  209.0 2.1 select_add_fusion.5
  211.2 0.1 compare_select_fusion.5
  211.2 1.8 gather_fusion.1
  213.1 0.5 fusion.72
  213.6 0.1 dynamic_slice.84
  213.7 0.1 dynamic_slice.85
  213.7 3.7 select_add_fusion.5
  217.4 2.7 copy.19
  220.1 0.9 slice_bitcast_fusion.5
  221.0 4.6 %collective-permute-start.10 = (f32[128,512]{1,0:T(8,128)S(1)}, f32[128,512]{1,0:T(8,128)S(1)}, u32[]{:S(2)}, u32[]{:S(2)}) collective-permute-start(f32[128,512]{1,0:T(8,128)S(1)} %get-tuple-element.334), channel_id=1, source_target_pairs={{0,16},{8,24},{16,32},{24,40},{32,48},{40,56},{48,64},{56,72},{64,... | collective-permute-start | bytes 786440 | tf_op jit(solution)/shard_map/ppermute | solution.py:12
  225.7 6.0 %collective-permute-start.11 = (f32[128,512]{1,0:T(8,128)}, f32[128,512]{1,0:T(8,128)S(1)}, u32[]{:S(2)}, u32[]{:S(2)}) collective-permute-start(f32[128,512]{1,0:T(8,128)} %get-tuple-element.333), channel_id=1, source_target_pairs={{0,24},{8,32},{16,40},{24,48},{32,56},{40,64},{48,72},{56,80},{64,... | collective-permute-start | bytes 786440 | tf_op jit(solution)/shard_map/ppermute | solution.py:12
  231.7 4.9 %collective-permute-start.6 = (f32[128,512]{1,0:T(8,128)}, f32[128,512]{1,0:T(8,128)}, u32[]{:S(2)}, u32[]{:S(2)}) collective-permute-start(f32[128,512]{1,0:T(8,128)} %get-tuple-element.332), channel_id=1, source_target_pairs={{24,0},{32,8},{40,16},{48,24},{56,32},{64,40},{72,48},{80,56},{88,... | collective-permute-start | bytes 786440 | tf_op jit(solution)/shard_map/ppermute | solution.py:12
  236.7 3.3 collective-permute-start.7
  240.0 2.5 collective-permute-start.8
  242.5 2.8 collective-permute-done.10
  245.3 1.9 collective-permute-start.9
  247.3 13.2 %psum.30 = f32[512]{0:T(512)S(1)} all-reduce(f32[512]{0:T(512)S(1)} %get-tuple-element.330), channel_id=1, replica_groups=mesh['row'=64,'col'=8] {'col'}, use_global_device_ids=true, to_apply=%region_6.0 | all-reduce | flops 512 | bytes 4096 | tf_op jit(solution)/shard_map/psum | solution.py:77
  260.5 158.8 %psum.31 = f32[512]{0:T(512)} all-reduce(f32[512]{0:T(512)S(1)} %psum.30), channel_id=1, replica_groups=mesh['row'=64,'col'=8] {'row'}, use_global_device_ids=true, to_apply=%region_7.0 | all-reduce | flops 512 | bytes 4096 | tf_op jit(solution)/shard_map/psum | solution.py:77
  419.4 2.0 fusion.42
  421.4 2.3 copy.61
  (33 shorter events, 0.1 us)
Async XLA Ops:
  7.2 92.8 %copy-start = (bf16[512,512]{1,0:T(8,128)(2,1)S(1)}, bf16[512,512]{1,0:T(8,128)(2,1)}, u32[]{:S(2)}) copy-start(bf16[512,512]{1,0:T(8,128)(2,1)} %param.12) | copy-start | bytes 1572868
  7.2 92.8 %reduce-scatter.2.cloned.1.call-start = ((), (), s32[]{:S(2)}) async-start(), calls=%async_computation.1 | async-start | bytes 2359296 | tf_op jit(solution)/shard_map/reduce_scatter | solution.py:64
  7.2 27.0 %collective-permute-start = (bf16[128,512]{1,0:T(8,128)(2,1)}, bf16[128,512]{1,0:T(8,128)(2,1)S(1)}, u32[]{:S(2)}, u32[]{:S(2)}) collective-permute-start(bf16[128,512]{1,0:T(8,128)(2,1)} %param.11), channel_id=1, source_target_pairs={{0,24},{8,32},{16,40},{24,48},{32,56},{40,64},{48,72},{56,80},{64,... | collective-permute-start | bytes 393224 | tf_op jit(solution)/shard_map/ppermute | solution.py:12
  15.3 22.0 %collective-permute-start.1 = (bf16[128,512]{1,0:T(8,128)(2,1)}, bf16[128,512]{1,0:T(8,128)(2,1)S(1)}, u32[]{:S(2)}, u32[]{:S(2)}) collective-permute-start(bf16[128,512]{1,0:T(8,128)(2,1)} %param.11), channel_id=1, source_target_pairs={{0,16},{8,24},{16,32},{24,40},{32,48},{40,56},{48,64},{56,72},{64,... | collective-permute-start | bytes 393224 | tf_op jit(solution)/shard_map/ppermute | solution.py:12
  21.7 15.6 %collective-permute-start.2 = (bf16[128,512]{1,0:T(8,128)(2,1)}, bf16[128,512]{1,0:T(8,128)(2,1)S(1)}, u32[]{:S(2)}, u32[]{:S(2)}) collective-permute-start(bf16[128,512]{1,0:T(8,128)(2,1)} %param.11), channel_id=1, source_target_pairs={{0,8},{8,16},{16,24},{24,32},{32,40},{40,48},{48,56},{56,64},{64,7... | collective-permute-start | bytes 393224 | tf_op jit(solution)/shard_map/ppermute | solution.py:12
  25.1 13.1 %collective-permute-start.3 = (bf16[128,512]{1,0:T(8,128)(2,1)}, bf16[128,512]{1,0:T(8,128)(2,1)S(1)}, u32[]{:S(2)}, u32[]{:S(2)}) collective-permute-start(bf16[128,512]{1,0:T(8,128)(2,1)} %param.11), channel_id=1, source_target_pairs={{8,0},{16,8},{24,16},{32,24},{40,32},{48,40},{56,48},{64,56},{72,6... | collective-permute-start | bytes 393224 | tf_op jit(solution)/shard_map/ppermute | solution.py:12
  30.9 19.6 %collective-permute-start.4 = (bf16[128,512]{1,0:T(8,128)(2,1)}, bf16[128,512]{1,0:T(8,128)(2,1)S(1)}, u32[]{:S(2)}, u32[]{:S(2)}) collective-permute-start(bf16[128,512]{1,0:T(8,128)(2,1)} %param.11), channel_id=1, source_target_pairs={{16,0},{24,8},{32,16},{40,24},{48,32},{56,40},{64,48},{72,56},{80,... | collective-permute-start | bytes 393224 | tf_op jit(solution)/shard_map/ppermute | solution.py:12
  34.2 16.3 %collective-permute-start.5 = (bf16[128,512]{1,0:T(8,128)(2,1)}, bf16[128,512]{1,0:T(8,128)(2,1)S(1)}, u32[]{:S(2)}, u32[]{:S(2)}) collective-permute-start(bf16[128,512]{1,0:T(8,128)(2,1)} %param.11), channel_id=1, source_target_pairs={{24,0},{32,8},{40,16},{48,24},{56,32},{64,40},{72,48},{80,56},{88,... | collective-permute-start | bytes 393224 | tf_op jit(solution)/shard_map/ppermute | solution.py:12
  64.9 35.0 %copy-start.3 = (bf16[128,512]{1,0:T(8,128)(2,1)S(1)}, bf16[128,512]{1,0:T(8,128)(2,1)}, u32[]{:S(2)}) copy-start(bf16[128,512]{1,0:T(8,128)(2,1)} %param.17) | copy-start | bytes 393220
  65.0 35.0 %copy-start.4 = (f32[512]{0:T(512)S(1)}, f32[512]{0:T(512)}, u32[]{:S(2)}) copy-start(f32[512]{0:T(512)} %param.13) | copy-start | bytes 6148
  65.0 110.6 %all-reduce.3.cloned.1.call-start = ((), (), s32[]{:S(2)}) async-start(), calls=%async_computation.2 | async-start | bytes 2097152 | tf_op jit(solution)/shard_map/psum | solution.py:77
  100.0 2.1 copy-start.2
  102.1 104.3 %copy-start.1 = (bf16[16,128,128]{2,1,0:T(8,128)(2,1)S(1)}, bf16[16,128,128]{2,1,0:T(8,128)(2,1)}, u32[]{:S(2)}) copy-start(bf16[16,128,128]{2,1,0:T(8,128)(2,1)} %get-tuple-element.502) | copy-start | bytes 1572868
  103.4 103.0 %all-gather.2.cloned.1.call-start = ((), (), s32[]{:S(2)}) async-start(), calls=%async_computation.4 | async-start | bytes 1179648 | tf_op jit(solution)/shard_map/all_gather | solution.py:81
  104.5 316.9 %all-reduce.5.cloned.1.call-start = ((), (), s32[]{:S(2)}) async-start(), calls=%async_computation.3 | async-start | bytes 2097152 | tf_op jit(solution)/shard_map/psum | solution.py:77
  221.0 24.3 %collective-permute-start.10 = (f32[128,512]{1,0:T(8,128)S(1)}, f32[128,512]{1,0:T(8,128)S(1)}, u32[]{:S(2)}, u32[]{:S(2)}) collective-permute-start(f32[128,512]{1,0:T(8,128)S(1)} %get-tuple-element.334), channel_id=1, source_target_pairs={{0,16},{8,24},{16,32},{24,40},{32,48},{40,56},{48,64},{56,72},{64,... | collective-permute-start | bytes 786440 | tf_op jit(solution)/shard_map/ppermute | solution.py:12
  225.7 193.7 %collective-permute-start.11 = (f32[128,512]{1,0:T(8,128)}, f32[128,512]{1,0:T(8,128)S(1)}, u32[]{:S(2)}, u32[]{:S(2)}) collective-permute-start(f32[128,512]{1,0:T(8,128)} %get-tuple-element.333), channel_id=1, source_target_pairs={{0,24},{8,32},{16,40},{24,48},{32,56},{40,64},{48,72},{56,80},{64,... | collective-permute-start | bytes 786440 | tf_op jit(solution)/shard_map/ppermute | solution.py:12
  231.7 187.6 %collective-permute-start.6 = (f32[128,512]{1,0:T(8,128)}, f32[128,512]{1,0:T(8,128)}, u32[]{:S(2)}, u32[]{:S(2)}) collective-permute-start(f32[128,512]{1,0:T(8,128)} %get-tuple-element.332), channel_id=1, source_target_pairs={{24,0},{32,8},{40,16},{48,24},{56,32},{64,40},{72,48},{80,56},{88,... | collective-permute-start | bytes 786440 | tf_op jit(solution)/shard_map/ppermute | solution.py:12
  236.7 182.7 %collective-permute-start.7 = (f32[128,512]{1,0:T(8,128)}, f32[128,512]{1,0:T(8,128)}, u32[]{:S(2)}, u32[]{:S(2)}) collective-permute-start(f32[128,512]{1,0:T(8,128)} %get-tuple-element.337), channel_id=1, source_target_pairs={{16,0},{24,8},{32,16},{40,24},{48,32},{56,40},{64,48},{72,56},{80,... | collective-permute-start | bytes 786440 | tf_op jit(solution)/shard_map/ppermute | solution.py:12
  240.0 179.4 %collective-permute-start.8 = (f32[128,512]{1,0:T(8,128)S(1)}, f32[128,512]{1,0:T(8,128)}, u32[]{:S(2)}, u32[]{:S(2)}) collective-permute-start(f32[128,512]{1,0:T(8,128)S(1)} %get-tuple-element.336), channel_id=1, source_target_pairs={{8,0},{16,8},{24,16},{32,24},{40,32},{48,40},{56,48},{64,56},{72,6... | collective-permute-start | bytes 786440 | tf_op jit(solution)/shard_map/ppermute | solution.py:12
  245.3 174.0 %collective-permute-start.9 = (f32[128,512]{1,0:T(8,128)S(1)}, f32[128,512]{1,0:T(8,128)}, u32[]{:S(2)}, u32[]{:S(2)}) collective-permute-start(f32[128,512]{1,0:T(8,128)S(1)} %get-tuple-element.335), channel_id=1, source_target_pairs={{0,8},{8,16},{16,24},{24,32},{32,40},{40,48},{48,56},{56,64},{64,7... | collective-permute-start | bytes 786440 | tf_op jit(solution)/shard_map/ppermute | solution.py:12
Sparse Core Ops, SparseCore 0:
  65.1 34.8 reduce-scatter.1
  103.5 72.0 all-reduce.2
  178.4 28.0 all-gather.1
  209.5 198.9 all-reduce.4
